TPU v7x, 32 devices: a whole 2x2x4 slice. The times are simulated.
32 devices in a mesh: outer: 4 (over y, x), inner: 8 (over z, core).
Axes of the slice: x: 2, y: 2, z: 4, core: 2. Of those that a mesh axis runs over, the one named last changes fastest.
Arguments:
- shocks: float32 [32, 2, 60, 1024], P('outer', None, None, 'inner'), may hold values from -5 to 5, as said below
- node_rate: float32 [32, 2], P('outer'), may hold values from -0.025 to 0.06
- ladder_rung: int32 [32, 2], P('outer'), may hold values from 0 to 3
- cash_flows: float32 [60, 192], replicated, may hold values from 0.005 to 0.05
- owner_map: int32 [192], replicated, may hold values from 0 to 191, each once
- capital: float32 [32, 192], P('outer', 'inner'), may hold values from 0.3 to 1.5
Outputs:
- cohort_value: float32 [32, 2, 192], P('outer', None, 'inner')
- cohort_downside: float32 [32, 2, 192], P('outer', None, 'inner')
- fund_indexation: float32 [32, 2], P('outer')
- cohort_summary: float32 [2, 192], P(None, 'inner')
Inputs may be any that keep to these rules, and one draw needn't show every extreme that they name: shocks of the inner short rate, one per path, year, date and scenario. Slot j holds cohort owner_map[j]; every cohort is held in exactly one slot.
All inputs are finite; a program needn't handle non-finite values.
Results may differ from a plain program's by a relative error of at most 0.0001.
Values sent between devices are 32-bit elements; how exact they have to be, the bound alone decides.
A program may use at most 64 MiB of HBM per device.

v0:
```python
from functools import partial

import jax
import jax.numpy as jnp
from jax import lax
from jax.sharding import PartitionSpec as P

DATES = 2


REVERT = 0.05
LONG_LEVEL = 0.025
VOLATILITY = 0.01
EPSILON = 1e-06


def year_tables(year_count):
    year_index = jnp.arange(year_count, dtype=jnp.float32)
    later_year = year_index[None, :]
    early_year = year_index[:, None]
    decay_rate = 1.0 - REVERT
    weights = jnp.where(
        early_year <= later_year,
        (1.0 - jnp.power(decay_rate, later_year + 1.0 - early_year)) / REVERT,
        0.0,
    )
    counts = year_index + 1.0
    drift_ramp = decay_rate * (1.0 - jnp.power(decay_rate, counts)) / REVERT
    return (counts, drift_ramp, weights)


def discount(node_rates, shocks_now):
    counts, drift_ramp, weights = year_tables(shocks_now.shape[1])
    drift_part = (
        counts[None, :] * LONG_LEVEL + (node_rates[:, None] - LONG_LEVEL) * drift_ramp[None, :]
    )
    shock_sums = jnp.einsum("jk,sjp->skp", weights, shocks_now, precision=lax.Precision.HIGHEST)
    return jnp.exp(-(drift_part[:, :, None] + VOLATILITY * shock_sums))


def ladder(funding_ratio, rung_level):
    floor_level = 0.9 + 0.1 * rung_level
    full_index = 0.01 + 0.005 * rung_level
    return full_index * jnp.clip((funding_ratio - floor_level) / 0.4, 0.0, 1.0)


def scenario_value(slot_flows, pieces):
    disc_one, index_one = pieces
    year_count = jnp.arange(slot_flows.shape[0], dtype=jnp.float32) + 1.0
    growth = jnp.exp(year_count[:, None, None] * jnp.log1p(index_one)[None, :, :])
    return jnp.sum(slot_flows[:, :, None] * disc_one[:, None, :] * growth, axis=0)


def summarize(pieces):
    path_count = pieces.shape[2]
    mean_value = jnp.sum(pieces, axis=2) / path_count
    shortfall = jnp.minimum(pieces - mean_value[:, :, None], 0.0)
    return (mean_value, jnp.sqrt(jnp.sum(shortfall * shortfall, axis=2) / path_count + EPSILON))


def shards(shocks, node_rate, ladder_rung, cash_flows, owner_map, capital):
    groups = lax.axis_size("inner")
    path_total = shocks.shape[3] * groups
    cohort_ids = jnp.arange(cash_flows.shape[1], dtype=jnp.int32)
    picker = (cohort_ids[:, None] == owner_map[None, :]).astype(jnp.float32)
    slot_flows = jnp.dot(
        cash_flows, picker, precision=lax.Precision.HIGHEST, preferred_element_type=jnp.float32
    )
    holdings = lax.all_gather(capital, "inner", axis=1, tiled=True)
    values, spreads, fund_terms = ([], [], [])
    for date_index in range(DATES):
        discounts = discount(node_rate[:, date_index], shocks[:, date_index])
        nominal = jnp.einsum("kc,skp->scp", slot_flows, discounts, precision=lax.Precision.HIGHEST)
        rung_level = ladder_rung[:, date_index].astype(jnp.float32)
        fund_ratio = jnp.sum(holdings, axis=1)[:, None] / jnp.sum(nominal, axis=1)
        fund_share = jnp.sum(ladder(fund_ratio, rung_level[:, None]), axis=1)
        fund_terms.append(lax.psum(fund_share, "inner"))
        cohort_index = ladder(holdings[:, :, None] / nominal, rung_level[:, None, None])
        indexed = lax.map(partial(scenario_value, slot_flows), (discounts, cohort_index))
        mean_own, spread_own = summarize(
            lax.all_to_all(indexed, "inner", split_axis=1, concat_axis=2, tiled=True)
        )
        if date_index + 1 < DATES:
            holdings = lax.all_gather(mean_own, "inner", axis=1, tiled=True)
        values.append(mean_own)
        spreads.append(spread_own)
    fund_stack = jnp.stack(fund_terms, axis=1)
    fund_indexation = 100.0 * fund_stack / path_total
    cohort_value = jnp.stack(values, axis=1)
    cohort_downside = jnp.stack(spreads, axis=1)
    scenario_total = cohort_value.shape[0] * lax.axis_size("outer")
    cohort_summary = lax.psum(jnp.sum(cohort_value, axis=0), "outer") / scenario_total
    return (cohort_value, cohort_downside, fund_indexation, cohort_summary)


def solution(mesh):
    return jax.shard_map(
        shards,
        mesh=mesh,
        in_specs=(
            P("outer", None, None, "inner"),
            P("outer", None),
            P("outer", None),
            P(),
            P(),
            P("outer", "inner"),
        ),
        out_specs=(
            P("outer", None, "inner"),
            P("outer", None, "inner"),
            P("outer", None),
            P(None, "inner"),
        ),
        check_vma=False,
    )
```

profile of v0, /device:TPU:0, one launch (start us, length us, event | category | flops | bytes accessed | tf_op | source)
XLA Modules:
  0.0 206.3 jit_solution(14808606731141975090)
XLA Ops:
  0.7 0.8 add_bitcast_fusion.5
  1.4 0.8 add_bitcast_fusion.1
  2.2 15.8 %all-gather = f32[8,24,8]{1,2,0:T(8,128)S(1)} all-gather(f32[1,24,8]{1,2,0:T(8,128)} %bitcast.120), channel_id=1, replica_groups=mesh['outer'=4,'inner'=8] {'inner'}, dimensions={0}, use_global_device_ids=true | all-gather | bytes 6912 | tf_op jit(solution)/shard_map/all_gather | solution.py:69
  18.1 1.7 fusion.43
  20.6 1.0 fusion.41
  21.6 0.9 broadcast.313.clone2
  22.5 50.0 %while.20 = (s32[]{:T(128)}, f32[8,192,128]{2,0,1:T(8,128)}, f32[60,192]{1,0:T(8,128)S(1)}, f32[8,60,128]{2,1,0:T(8,128)S(1)}, f32[8,192,128]{2,1,0:T(8,128)S(1)}, /*index=5*/s32[]{:T(128)}, s32[]{:T(128)}) while((s32[]{:T(128)}, f32[8,192,128]{2,0,1:T(8,128)}, f32[60,192]{1,0:T(8,128)S(1)}, f32[8,60,128]{2,1,0:T(8,128)S(1)}, ...), condition=%wide.region_2.3_spmd, body=%wide.region_0.0_spmd.sunk | while | flops 5873726 | bytes 728641 | solution.py:79
  22.5 2.2 %multiply_reduce_fusion.8 = f32[192,128]{1,0:T(8,128)S(1)} fusion(f32[192,128]{1,0:T(8,128)S(1)} %log-plus-one_bitcast_fusion.4, f32[60]{0:T(128)S(1)} %iota_add_fusion.5, f32[60,128]{1,0:T(8,128)S(1)} %dynamic-slice_bitcast_fusion.4, f32[60,192]{1,0:T(8,128)S(1)} %get-tuple-element.207), kind=kLoop, calls=%fused_computation.clone.1 | loop fusion | flops 5873664 | bytes 273648 | tf_op jit(solution)/shard_map/while/body/eval_jaxpr/reduce_sum | solution.py:51
  24.8 4.0 %dynamic_update_slice.9 = f32[8,192,128]{2,0,1:T(8,128)} dynamic-update-slice(f32[8,192,128]{2,0,1:T(8,128)} %get-tuple-element.199, f32[1,192,128]{2,0,1:T(1,128)S(1)} %bitcast.114, s32[]{:T(128)S(6)} %copy.90, s32[]{:T(128)} %constant.37.clone.1..sunk, s32[]{:T(128)} %constant.37.clone.1..sunk) | dynamic-update-slice | bytes 196612 | tf_op jit(solution)/shard_map/while/body/jit(dynamic_update_index_in_dim)/dynamic_update_slice | solution.py:79
  28.8 2.2 %multiply_reduce_fusion.8 = f32[192,128]{1,0:T(8,128)S(1)} fusion(f32[192,128]{1,0:T(8,128)S(1)} %log-plus-one_bitcast_fusion.4, f32[60]{0:T(128)S(1)} %iota_add_fusion.5, f32[60,128]{1,0:T(8,128)S(1)} %dynamic-slice_bitcast_fusion.4, f32[60,192]{1,0:T(8,128)S(1)} %get-tuple-element.207), kind=kLoop, calls=%fused_computation.clone.1 | loop fusion | flops 5873664 | bytes 273648 | tf_op jit(solution)/shard_map/while/body/eval_jaxpr/reduce_sum | solution.py:51
  31.0 4.0 %dynamic_update_slice.9 = f32[8,192,128]{2,0,1:T(8,128)} dynamic-update-slice(f32[8,192,128]{2,0,1:T(8,128)} %get-tuple-element.199, f32[1,192,128]{2,0,1:T(1,128)S(1)} %bitcast.114, s32[]{:T(128)S(6)} %copy.90, s32[]{:T(128)} %constant.37.clone.1..sunk, s32[]{:T(128)} %constant.37.clone.1..sunk) | dynamic-update-slice | bytes 196612 | tf_op jit(solution)/shard_map/while/body/jit(dynamic_update_index_in_dim)/dynamic_update_slice | solution.py:79
  35.1 2.2 %multiply_reduce_fusion.8 = f32[192,128]{1,0:T(8,128)S(1)} fusion(f32[192,128]{1,0:T(8,128)S(1)} %log-plus-one_bitcast_fusion.4, f32[60]{0:T(128)S(1)} %iota_add_fusion.5, f32[60,128]{1,0:T(8,128)S(1)} %dynamic-slice_bitcast_fusion.4, f32[60,192]{1,0:T(8,128)S(1)} %get-tuple-element.207), kind=kLoop, calls=%fused_computation.clone.1 | loop fusion | flops 5873664 | bytes 273648 | tf_op jit(solution)/shard_map/while/body/eval_jaxpr/reduce_sum | solution.py:51
  37.3 4.0 %dynamic_update_slice.9 = f32[8,192,128]{2,0,1:T(8,128)} dynamic-update-slice(f32[8,192,128]{2,0,1:T(8,128)} %get-tuple-element.199, f32[1,192,128]{2,0,1:T(1,128)S(1)} %bitcast.114, s32[]{:T(128)S(6)} %copy.90, s32[]{:T(128)} %constant.37.clone.1..sunk, s32[]{:T(128)} %constant.37.clone.1..sunk) | dynamic-update-slice | bytes 196612 | tf_op jit(solution)/shard_map/while/body/jit(dynamic_update_index_in_dim)/dynamic_update_slice | solution.py:79
  41.3 2.2 %multiply_reduce_fusion.8 = f32[192,128]{1,0:T(8,128)S(1)} fusion(f32[192,128]{1,0:T(8,128)S(1)} %log-plus-one_bitcast_fusion.4, f32[60]{0:T(128)S(1)} %iota_add_fusion.5, f32[60,128]{1,0:T(8,128)S(1)} %dynamic-slice_bitcast_fusion.4, f32[60,192]{1,0:T(8,128)S(1)} %get-tuple-element.207), kind=kLoop, calls=%fused_computation.clone.1 | loop fusion | flops 5873664 | bytes 273648 | tf_op jit(solution)/shard_map/while/body/eval_jaxpr/reduce_sum | solution.py:51
  43.6 4.0 %dynamic_update_slice.9 = f32[8,192,128]{2,0,1:T(8,128)} dynamic-update-slice(f32[8,192,128]{2,0,1:T(8,128)} %get-tuple-element.199, f32[1,192,128]{2,0,1:T(1,128)S(1)} %bitcast.114, s32[]{:T(128)S(6)} %copy.90, s32[]{:T(128)} %constant.37.clone.1..sunk, s32[]{:T(128)} %constant.37.clone.1..sunk) | dynamic-update-slice | bytes 196612 | tf_op jit(solution)/shard_map/while/body/jit(dynamic_update_index_in_dim)/dynamic_update_slice | solution.py:79
  47.6 2.2 %multiply_reduce_fusion.8 = f32[192,128]{1,0:T(8,128)S(1)} fusion(f32[192,128]{1,0:T(8,128)S(1)} %log-plus-one_bitcast_fusion.4, f32[60]{0:T(128)S(1)} %iota_add_fusion.5, f32[60,128]{1,0:T(8,128)S(1)} %dynamic-slice_bitcast_fusion.4, f32[60,192]{1,0:T(8,128)S(1)} %get-tuple-element.207), kind=kLoop, calls=%fused_computation.clone.1 | loop fusion | flops 5873664 | bytes 273648 | tf_op jit(solution)/shard_map/while/body/eval_jaxpr/reduce_sum | solution.py:51
  49.8 4.0 %dynamic_update_slice.9 = f32[8,192,128]{2,0,1:T(8,128)} dynamic-update-slice(f32[8,192,128]{2,0,1:T(8,128)} %get-tuple-element.199, f32[1,192,128]{2,0,1:T(1,128)S(1)} %bitcast.114, s32[]{:T(128)S(6)} %copy.90, s32[]{:T(128)} %constant.37.clone.1..sunk, s32[]{:T(128)} %constant.37.clone.1..sunk) | dynamic-update-slice | bytes 196612 | tf_op jit(solution)/shard_map/while/body/jit(dynamic_update_index_in_dim)/dynamic_update_slice | solution.py:79
  53.8 2.2 %multiply_reduce_fusion.8 = f32[192,128]{1,0:T(8,128)S(1)} fusion(f32[192,128]{1,0:T(8,128)S(1)} %log-plus-one_bitcast_fusion.4, f32[60]{0:T(128)S(1)} %iota_add_fusion.5, f32[60,128]{1,0:T(8,128)S(1)} %dynamic-slice_bitcast_fusion.4, f32[60,192]{1,0:T(8,128)S(1)} %get-tuple-element.207), kind=kLoop, calls=%fused_computation.clone.1 | loop fusion | flops 5873664 | bytes 273648 | tf_op jit(solution)/shard_map/while/body/eval_jaxpr/reduce_sum | solution.py:51
  56.1 4.0 %dynamic_update_slice.9 = f32[8,192,128]{2,0,1:T(8,128)} dynamic-update-slice(f32[8,192,128]{2,0,1:T(8,128)} %get-tuple-element.199, f32[1,192,128]{2,0,1:T(1,128)S(1)} %bitcast.114, s32[]{:T(128)S(6)} %copy.90, s32[]{:T(128)} %constant.37.clone.1..sunk, s32[]{:T(128)} %constant.37.clone.1..sunk) | dynamic-update-slice | bytes 196612 | tf_op jit(solution)/shard_map/while/body/jit(dynamic_update_index_in_dim)/dynamic_update_slice | solution.py:79
  60.1 2.2 %multiply_reduce_fusion.8 = f32[192,128]{1,0:T(8,128)S(1)} fusion(f32[192,128]{1,0:T(8,128)S(1)} %log-plus-one_bitcast_fusion.4, f32[60]{0:T(128)S(1)} %iota_add_fusion.5, f32[60,128]{1,0:T(8,128)S(1)} %dynamic-slice_bitcast_fusion.4, f32[60,192]{1,0:T(8,128)S(1)} %get-tuple-element.207), kind=kLoop, calls=%fused_computation.clone.1 | loop fusion | flops 5873664 | bytes 273648 | tf_op jit(solution)/shard_map/while/body/eval_jaxpr/reduce_sum | solution.py:51
  62.3 4.0 %dynamic_update_slice.9 = f32[8,192,128]{2,0,1:T(8,128)} dynamic-update-slice(f32[8,192,128]{2,0,1:T(8,128)} %get-tuple-element.199, f32[1,192,128]{2,0,1:T(1,128)S(1)} %bitcast.114, s32[]{:T(128)S(6)} %copy.90, s32[]{:T(128)} %constant.37.clone.1..sunk, s32[]{:T(128)} %constant.37.clone.1..sunk) | dynamic-update-slice | bytes 196612 | tf_op jit(solution)/shard_map/while/body/jit(dynamic_update_index_in_dim)/dynamic_update_slice | solution.py:79
  66.3 2.2 %multiply_reduce_fusion.8 = f32[192,128]{1,0:T(8,128)S(1)} fusion(f32[192,128]{1,0:T(8,128)S(1)} %log-plus-one_bitcast_fusion.4, f32[60]{0:T(128)S(1)} %iota_add_fusion.5, f32[60,128]{1,0:T(8,128)S(1)} %dynamic-slice_bitcast_fusion.4, f32[60,192]{1,0:T(8,128)S(1)} %get-tuple-element.207), kind=kLoop, calls=%fused_computation.clone.1 | loop fusion | flops 5873664 | bytes 273648 | tf_op jit(solution)/shard_map/while/body/eval_jaxpr/reduce_sum | solution.py:51
  68.6 4.0 %dynamic_update_slice.9 = f32[8,192,128]{2,0,1:T(8,128)} dynamic-update-slice(f32[8,192,128]{2,0,1:T(8,128)} %get-tuple-element.199, f32[1,192,128]{2,0,1:T(1,128)S(1)} %bitcast.114, s32[]{:T(128)S(6)} %copy.90, s32[]{:T(128)} %constant.37.clone.1..sunk, s32[]{:T(128)} %constant.37.clone.1..sunk) | dynamic-update-slice | bytes 196612 | tf_op jit(solution)/shard_map/while/body/jit(dynamic_update_index_in_dim)/dynamic_update_slice | solution.py:79
  72.5 4.6 %all-to-all-start = ((f32[8,192,128]{2,0,1:T(8,128)}), f32[8,192,128]{2,0,1:T(8,128)S(1)}, u32[]{:S(2)}, u32[]{:S(2)}) async-start(f32[8,192,128]{2,0,1:T(8,128)} %get-tuple-element.58), calls=%async_computation | async-start | bytes 1572864 | tf_op jit(solution)/shard_map/all_to_all | solution.py:81
  77.6 20.5 %all-to-all-done = f32[8,192,128]{2,0,1:T(8,128)S(1)} async-done(((f32[8,192,128]{2,0,1:T(8,128)}), f32[8,192,128]{2,0,1:T(8,128)S(1)}, u32[]{:S(2)}, u32[]{:S(2)}) %all-to-all-start) | async-done | bytes 786464 | tf_op jit(solution)/shard_map/all_to_all | solution.py:81
  98.3 14.0 %all-gather.1 = f32[8,24,8]{1,2,0:T(8,128)S(1)} all-gather(f32[1,24,8]{1,2,0:T(8,128)S(1)} %copy.56), channel_id=1, replica_groups=mesh['outer'=4,'inner'=8] {'inner'}, dimensions={0}, use_global_device_ids=true | all-gather | bytes 6912 | tf_op jit(solution)/shard_map/all_gather | solution.py:84
  112.4 1.0 fusion.42
  113.4 0.9 broadcast.313.clone
  114.3 50.1 %while.21 = (s32[]{:T(128)}, f32[8,192,128]{2,0,1:T(8,128)}, f32[60,192]{1,0:T(8,128)S(1)}, f32[8,60,128]{2,1,0:T(8,128)S(1)}, f32[8,192,128]{2,1,0:T(8,128)S(1)}, /*index=5*/s32[]{:T(128)}, s32[]{:T(128)}) while((s32[]{:T(128)}, f32[8,192,128]{2,0,1:T(8,128)}, f32[60,192]{1,0:T(8,128)S(1)}, f32[8,60,128]{2,1,0:T(8,128)S(1)}, ...), condition=%wide.region_6.7_spmd, body=%wide.region_4.6_spmd.sunk | while | flops 5873726 | bytes 728641 | solution.py:79
  114.4 2.2 %multiply_reduce_fusion.9 = f32[192,128]{1,0:T(8,128)S(1)} fusion(f32[192,128]{1,0:T(8,128)S(1)} %log-plus-one_bitcast_fusion.5, f32[60]{0:T(128)S(1)} %iota_add_fusion.6, f32[60,128]{1,0:T(8,128)S(1)} %dynamic-slice_bitcast_fusion.5, f32[60,192]{1,0:T(8,128)S(1)} %get-tuple-element.228), kind=kLoop, calls=%fused_computation.4.clone.1 | loop fusion | flops 5873664 | bytes 273648 | tf_op jit(solution)/shard_map/while/body/eval_jaxpr/reduce_sum | solution.py:51
  116.6 4.0 %dynamic_update_slice.10 = f32[8,192,128]{2,0,1:T(8,128)} dynamic-update-slice(f32[8,192,128]{2,0,1:T(8,128)} %get-tuple-element.220, f32[1,192,128]{2,0,1:T(1,128)S(1)} %bitcast.115, s32[]{:T(128)S(6)} %copy.96, s32[]{:T(128)} %constant.37.clone.1..sunk.1, s32[]{:T(128)} %constant.37.clone.1..sunk.1) | dynamic-update-slice | bytes 196612 | tf_op jit(solution)/shard_map/while/body/jit(dynamic_update_index_in_dim)/dynamic_update_slice | solution.py:79
  120.7 2.2 %multiply_reduce_fusion.9 = f32[192,128]{1,0:T(8,128)S(1)} fusion(f32[192,128]{1,0:T(8,128)S(1)} %log-plus-one_bitcast_fusion.5, f32[60]{0:T(128)S(1)} %iota_add_fusion.6, f32[60,128]{1,0:T(8,128)S(1)} %dynamic-slice_bitcast_fusion.5, f32[60,192]{1,0:T(8,128)S(1)} %get-tuple-element.228), kind=kLoop, calls=%fused_computation.4.clone.1 | loop fusion | flops 5873664 | bytes 273648 | tf_op jit(solution)/shard_map/while/body/eval_jaxpr/reduce_sum | solution.py:51
  122.9 4.0 %dynamic_update_slice.10 = f32[8,192,128]{2,0,1:T(8,128)} dynamic-update-slice(f32[8,192,128]{2,0,1:T(8,128)} %get-tuple-element.220, f32[1,192,128]{2,0,1:T(1,128)S(1)} %bitcast.115, s32[]{:T(128)S(6)} %copy.96, s32[]{:T(128)} %constant.37.clone.1..sunk.1, s32[]{:T(128)} %constant.37.clone.1..sunk.1) | dynamic-update-slice | bytes 196612 | tf_op jit(solution)/shard_map/while/body/jit(dynamic_update_index_in_dim)/dynamic_update_slice | solution.py:79
  126.9 2.2 %multiply_reduce_fusion.9 = f32[192,128]{1,0:T(8,128)S(1)} fusion(f32[192,128]{1,0:T(8,128)S(1)} %log-plus-one_bitcast_fusion.5, f32[60]{0:T(128)S(1)} %iota_add_fusion.6, f32[60,128]{1,0:T(8,128)S(1)} %dynamic-slice_bitcast_fusion.5, f32[60,192]{1,0:T(8,128)S(1)} %get-tuple-element.228), kind=kLoop, calls=%fused_computation.4.clone.1 | loop fusion | flops 5873664 | bytes 273648 | tf_op jit(solution)/shard_map/while/body/eval_jaxpr/reduce_sum | solution.py:51
  129.1 4.0 %dynamic_update_slice.10 = f32[8,192,128]{2,0,1:T(8,128)} dynamic-update-slice(f32[8,192,128]{2,0,1:T(8,128)} %get-tuple-element.220, f32[1,192,128]{2,0,1:T(1,128)S(1)} %bitcast.115, s32[]{:T(128)S(6)} %copy.96, s32[]{:T(128)} %constant.37.clone.1..sunk.1, s32[]{:T(128)} %constant.37.clone.1..sunk.1) | dynamic-update-slice | bytes 196612 | tf_op jit(solution)/shard_map/while/body/jit(dynamic_update_index_in_dim)/dynamic_update_slice | solution.py:79
  133.2 2.2 %multiply_reduce_fusion.9 = f32[192,128]{1,0:T(8,128)S(1)} fusion(f32[192,128]{1,0:T(8,128)S(1)} %log-plus-one_bitcast_fusion.5, f32[60]{0:T(128)S(1)} %iota_add_fusion.6, f32[60,128]{1,0:T(8,128)S(1)} %dynamic-slice_bitcast_fusion.5, f32[60,192]{1,0:T(8,128)S(1)} %get-tuple-element.228), kind=kLoop, calls=%fused_computation.4.clone.1 | loop fusion | flops 5873664 | bytes 273648 | tf_op jit(solution)/shard_map/while/body/eval_jaxpr/reduce_sum | solution.py:51
  135.4 4.0 %dynamic_update_slice.10 = f32[8,192,128]{2,0,1:T(8,128)} dynamic-update-slice(f32[8,192,128]{2,0,1:T(8,128)} %get-tuple-element.220, f32[1,192,128]{2,0,1:T(1,128)S(1)} %bitcast.115, s32[]{:T(128)S(6)} %copy.96, s32[]{:T(128)} %constant.37.clone.1..sunk.1, s32[]{:T(128)} %constant.37.clone.1..sunk.1) | dynamic-update-slice | bytes 196612 | tf_op jit(solution)/shard_map/while/body/jit(dynamic_update_index_in_dim)/dynamic_update_slice | solution.py:79
  139.4 2.2 %multiply_reduce_fusion.9 = f32[192,128]{1,0:T(8,128)S(1)} fusion(f32[192,128]{1,0:T(8,128)S(1)} %log-plus-one_bitcast_fusion.5, f32[60]{0:T(128)S(1)} %iota_add_fusion.6, f32[60,128]{1,0:T(8,128)S(1)} %dynamic-slice_bitcast_fusion.5, f32[60,192]{1,0:T(8,128)S(1)} %get-tuple-element.228), kind=kLoop, calls=%fused_computation.4.clone.1 | loop fusion | flops 5873664 | bytes 273648 | tf_op jit(solution)/shard_map/while/body/eval_jaxpr/reduce_sum | solution.py:51
  141.7 4.0 %dynamic_update_slice.10 = f32[8,192,128]{2,0,1:T(8,128)} dynamic-update-slice(f32[8,192,128]{2,0,1:T(8,128)} %get-tuple-element.220, f32[1,192,128]{2,0,1:T(1,128)S(1)} %bitcast.115, s32[]{:T(128)S(6)} %copy.96, s32[]{:T(128)} %constant.37.clone.1..sunk.1, s32[]{:T(128)} %constant.37.clone.1..sunk.1) | dynamic-update-slice | bytes 196612 | tf_op jit(solution)/shard_map/while/body/jit(dynamic_update_index_in_dim)/dynamic_update_slice | solution.py:79
  145.7 2.2 %multiply_reduce_fusion.9 = f32[192,128]{1,0:T(8,128)S(1)} fusion(f32[192,128]{1,0:T(8,128)S(1)} %log-plus-one_bitcast_fusion.5, f32[60]{0:T(128)S(1)} %iota_add_fusion.6, f32[60,128]{1,0:T(8,128)S(1)} %dynamic-slice_bitcast_fusion.5, f32[60,192]{1,0:T(8,128)S(1)} %get-tuple-element.228), kind=kLoop, calls=%fused_computation.4.clone.1 | loop fusion | flops 5873664 | bytes 273648 | tf_op jit(solution)/shard_map/while/body/eval_jaxpr/reduce_sum | solution.py:51
  147.9 4.0 %dynamic_update_slice.10 = f32[8,192,128]{2,0,1:T(8,128)} dynamic-update-slice(f32[8,192,128]{2,0,1:T(8,128)} %get-tuple-element.220, f32[1,192,128]{2,0,1:T(1,128)S(1)} %bitcast.115, s32[]{:T(128)S(6)} %copy.96, s32[]{:T(128)} %constant.37.clone.1..sunk.1, s32[]{:T(128)} %constant.37.clone.1..sunk.1) | dynamic-update-slice | bytes 196612 | tf_op jit(solution)/shard_map/while/body/jit(dynamic_update_index_in_dim)/dynamic_update_slice | solution.py:79
  151.9 2.2 %multiply_reduce_fusion.9 = f32[192,128]{1,0:T(8,128)S(1)} fusion(f32[192,128]{1,0:T(8,128)S(1)} %log-plus-one_bitcast_fusion.5, f32[60]{0:T(128)S(1)} %iota_add_fusion.6, f32[60,128]{1,0:T(8,128)S(1)} %dynamic-slice_bitcast_fusion.5, f32[60,192]{1,0:T(8,128)S(1)} %get-tuple-element.228), kind=kLoop, calls=%fused_computation.4.clone.1 | loop fusion | flops 5873664 | bytes 273648 | tf_op jit(solution)/shard_map/while/body/eval_jaxpr/reduce_sum | solution.py:51
  154.2 4.0 %dynamic_update_slice.10 = f32[8,192,128]{2,0,1:T(8,128)} dynamic-update-slice(f32[8,192,128]{2,0,1:T(8,128)} %get-tuple-element.220, f32[1,192,128]{2,0,1:T(1,128)S(1)} %bitcast.115, s32[]{:T(128)S(6)} %copy.96, s32[]{:T(128)} %constant.37.clone.1..sunk.1, s32[]{:T(128)} %constant.37.clone.1..sunk.1) | dynamic-update-slice | bytes 196612 | tf_op jit(solution)/shard_map/while/body/jit(dynamic_update_index_in_dim)/dynamic_update_slice | solution.py:79
  158.2 2.2 %multiply_reduce_fusion.9 = f32[192,128]{1,0:T(8,128)S(1)} fusion(f32[192,128]{1,0:T(8,128)S(1)} %log-plus-one_bitcast_fusion.5, f32[60]{0:T(128)S(1)} %iota_add_fusion.6, f32[60,128]{1,0:T(8,128)S(1)} %dynamic-slice_bitcast_fusion.5, f32[60,192]{1,0:T(8,128)S(1)} %get-tuple-element.228), kind=kLoop, calls=%fused_computation.4.clone.1 | loop fusion | flops 5873664 | bytes 273648 | tf_op jit(solution)/shard_map/while/body/eval_jaxpr/reduce_sum | solution.py:51
  160.4 4.0 %dynamic_update_slice.10 = f32[8,192,128]{2,0,1:T(8,128)} dynamic-update-slice(f32[8,192,128]{2,0,1:T(8,128)} %get-tuple-element.220, f32[1,192,128]{2,0,1:T(1,128)S(1)} %bitcast.115, s32[]{:T(128)S(6)} %copy.96, s32[]{:T(128)} %constant.37.clone.1..sunk.1, s32[]{:T(128)} %constant.37.clone.1..sunk.1) | dynamic-update-slice | bytes 196612 | tf_op jit(solution)/shard_map/while/body/jit(dynamic_update_index_in_dim)/dynamic_update_slice | solution.py:79
  164.4 3.5 %all-to-all-start.1 = ((f32[8,192,128]{2,0,1:T(8,128)}), f32[8,192,128]{2,0,1:T(8,128)S(1)}, u32[]{:S(2)}, u32[]{:S(2)}) async-start(f32[8,192,128]{2,0,1:T(8,128)} %get-tuple-element.59), calls=%async_computation.1 | async-start | bytes 1572864 | tf_op jit(solution)/shard_map/all_to_all | solution.py:81
  168.6 24.5 %all-reduce = (f32[8,1]{0,1:T(1,128)S(1)}, f32[8,1]{0,1:T(1,128)S(1)}) all-reduce(f32[8,1]{0,1:T(1,128)S(1)} %bitcast.122, f32[8,1]{0,1:T(1,128)S(1)} %bitcast.121), channel_id=1, replica_groups=mesh['outer'=4,'inner'=8] {'inner'}, use_global_device_ids=true, to_apply=%region_17.18 | all-reduce | flops 16 | bytes 128 | tf_op jit(solution)/shard_map/psum | solution.py:77
  195.2 9.9 %psum.23 = f32[2,24]{1,0:T(2,128)S(1)} all-reduce(f32[2,24]{1,0:T(2,128)S(1)} %get-tuple-element.117), channel_id=1, replica_groups=mesh['outer'=4,'inner'=8] {'outer'}, use_global_device_ids=true, to_apply=%region_19.20 | all-reduce | flops 48 | bytes 384 | tf_op jit(solution)/shard_map/psum | solution.py:92
  (86 shorter events, 6.4 us)
Async XLA Ops:
  0.6 19.2 %copy-start = (f32[60,192]{1,0:T(8,128)S(1)}, f32[60,192]{1,0:T(8,128)}, u32[]{:S(2)}) copy-start(f32[60,192]{1,0:T(8,128)} %param.13) | copy-start | bytes 138244
  0.6 19.2 %copy-start.1 = (s32[192]{0:T(256)S(1)}, s32[192]{0:T(256)}, u32[]{:S(2)}) copy-start(s32[192]{0:T(256)} %param.14) | copy-start | bytes 2308
  72.5 25.6 %all-to-all-start = ((f32[8,192,128]{2,0,1:T(8,128)}), f32[8,192,128]{2,0,1:T(8,128)S(1)}, u32[]{:S(2)}, u32[]{:S(2)}) async-start(f32[8,192,128]{2,0,1:T(8,128)} %get-tuple-element.58), calls=%async_computation | async-start | bytes 1572864 | tf_op jit(solution)/shard_map/all_to_all | solution.py:81
  164.4 29.7 %all-to-all-start.1 = ((f32[8,192,128]{2,0,1:T(8,128)}), f32[8,192,128]{2,0,1:T(8,128)S(1)}, u32[]{:S(2)}, u32[]{:S(2)}) async-start(f32[8,192,128]{2,0,1:T(8,128)} %get-tuple-element.59), calls=%async_computation.1 | async-start | bytes 1572864 | tf_op jit(solution)/shard_map/all_to_all | solution.py:81
where the time goes:
time: 207 us; the launch traced here: 206 us
  local copies, waits for them, and re-layouts  69.4 us (34%)
  blocking collectives  64.2 us (31%)
  other arithmetic  39.9 us (19%)
  waiting for transfers between devices  20.5 us (10%)
  starting transfers between devices  8.17 us (4%)
  matrix products  3.07 us (1%)
    dynamic_update_slice x16, local copies, waits for them, and re-layouts, shards(): lax.map(partial(scenario_value, slot_flows), (discounts, cohort_index))  63.3 us
    reduce_sum x16, other arithmetic, scenario_value(): jnp.sum(slot_flows[:, :, None] * disc_one[:, None, :] * growth, axis=0)  35.6 us
    psum x1, blocking collectives, shards(): fund_terms.append(lax.psum(fund_share, 'inner'))  24.5 us
    all_to_all x2, waiting for transfers between devices, shards(): lax.all_to_all(indexed, 'inner', split_axis=1, concat_axis=2, tiled=True)  20.5 us
    all_gather x1, blocking collectives, shards(): holdings = lax.all_gather(capital, 'inner', axis=1, tiled=True)  15.8 us
    all_gather x1, blocking collectives, shards(): holdings = lax.all_gather(mean_own, 'inner', axis=1, tiled=True)  14 us
    psum x1, blocking collectives, shards(): lax.psum(jnp.sum(cohort_value, axis=0), 'outer') / scenario_total  9.91 us
    all_to_all x2, starting transfers between devices, shards(): lax.all_to_all(indexed, 'inner', split_axis=1, concat_axis=2, tiled=True)  8.17 us
  transfers between devices with their start and end apart: 2, of which 1 were waited for; matrix products, arithmetic and copies ran while one was open for 1% of the time, Pallas kernels for 0%

commit v1 on v0

v1 whole, which is shorter than its diff:
```python
from functools import partial

import jax
import jax.numpy as jnp
import ml_dtypes
import numpy as np
from jax import lax
from jax.experimental import pallas as pl
from jax.experimental.pallas import tpu as pltpu
from jax.sharding import PartitionSpec as P

MESH = pl.DeviceIdType.MESH
F32 = jnp.float32
BF16 = jnp.bfloat16

REVERT = 0.05
LONG_LEVEL = 0.025
VOLATILITY = 0.01
EPSILON = 1e-06
TOP_INDEX = 0.025


def split_bf16(table):
    high = table.astype(ml_dtypes.bfloat16)
    low = (table - high.astype(np.float64)).astype(ml_dtypes.bfloat16)
    return high, low


def discount_table(years, pad):
    decay = 1.0 - REVERT
    year = np.arange(years, dtype=np.float64)
    weights = np.where(
        year[:, None] <= year[None, :],
        (1.0 - decay ** np.maximum(year[None, :] + 1.0 - year[:, None], 0.0)) / REVERT,
        0.0,
    )
    count = year + 1.0
    ramp = decay * (1.0 - decay**count) / REVERT
    one = np.zeros((pad, pad))
    one[:years, :years] = -VOLATILITY * weights
    one[years, :years] = -LONG_LEVEL * (count - ramp)
    one[years + 1, :years] = -ramp
    high, low = split_bf16(one)
    rest = one - high.astype(np.float64) - low.astype(np.float64)
    one[years + 2] = rest[years]
    high, low = split_bf16(one)
    full = np.zeros((2, 4 * pad, 4 * pad), ml_dtypes.bfloat16)
    for which, part in enumerate((high, low)):
        for row in (0, 2 * pad):
            for copy in (0, pad):
                full[which, row : row + pad, copy : copy + pad] = part
                full[which, row + pad : row + 2 * pad, 2 * pad + copy : 3 * pad + copy] = part
    return full


def growth_table(years, pad):
    k = np.arange(years, dtype=np.float64) + 1.0
    probe = np.linspace(0.0, 1.0, 2001)
    exact = np.exp(k[:, None] * np.log1p(TOP_INDEX * probe)[None, :])
    for degree in range(3, 40):
        node = 0.5 + 0.5 * np.cos(np.pi * (np.arange(degree) + 0.5) / degree)
        quotient = np.expm1(k[:, None] * np.log1p(TOP_INDEX * node)[None, :]) / node
        cheb = np.polynomial.chebyshev.chebfit(2.0 * node - 1.0, quotient.T, degree - 1)
        table = np.zeros((degree + 1, years))
        table[0] = 1.0
        for i in range(years):
            line = np.polynomial.Chebyshev(cheb[:, i], domain=[0.0, 1.0]).convert(
                kind=np.polynomial.Polynomial, domain=[-1, 1], window=[-1, 1]
            )
            table[1 : 1 + len(line.coef), i] = line.coef
        found = np.zeros_like(exact)
        for m in range(degree, -1, -1):
            found = found * probe[None, :] + table[m][:, None]
        if np.max(np.abs(found / exact - 1.0)) < 2.0**-25:
            break
    out = np.zeros((degree + 1, pad, 128), np.float32)
    out[:, :years] = table[:, :, None]
    return out


def kernel(
    n_in, n_out, years, pad, cohorts, lanes, terms,
    rate_ref, rung_ref, shock_ref, flow_ref, owner_ref, capital_ref, weight_ref, growth_ref,
    value_ref, down_ref, fund_ref, summary_ref,
    lhs, gmat, coef, inverse, vals, hold, send, recv, sum_send, sum_recv,
    send_sem, recv_sem, osend_sem, orecv_sem,
):
    scen, dates, _, paths = shock_ref.shape
    own = capital_ref.shape[1]
    total = paths * n_in
    me = lax.axis_index("inner")
    me_out = lax.axis_index("outer")
    barrier = pltpu.get_barrier_semaphore()
    for o in range(1, n_in):
        pl.semaphore_signal(barrier, 1, device_id={"inner": lax.rem(me + o, n_in)}, device_id_type=MESH)
    for o in range(1, n_out):
        pl.semaphore_signal(barrier, 1, device_id={"outer": lax.rem(me_out + o, n_out)}, device_id_type=MESH)

    lane = lax.broadcasted_iota(jnp.int32, (scen, lanes), 1)
    is_slot = lane < cohorts

    def inner_copy(r, o):
        return pltpu.make_async_remote_copy(
            src_ref=send.at[r],
            dst_ref=recv.at[r, me],
            send_sem=send_sem.at[r, o - 1],
            recv_sem=recv_sem.at[r, o - 1],
            device_id={"inner": lax.rem(me + o, n_in)},
            device_id_type=MESH,
        )

    def start(r):
        for o in range(1, n_in):
            inner_copy(r, o).start()
        recv[r, me] = send[r]

    def finish(r):
        for o in range(1, n_in):
            inner_copy(r, o).wait_recv()
        out = recv[r, 0]
        for i in range(1, n_in):
            out = out + recv[r, i]
        return out

    def set_hold(held):
        fund = jnp.sum(jnp.where(is_slot, held, 0.0), axis=1, keepdims=True)
        hold[...] = jnp.where(is_slot, held, fund)

    def discounts(t):
        def body(i, carry):
            row4 = lax.broadcasted_iota(jnp.int32, (pad - years, paths), 0)
            parts = []
            for h in range(2):
                s = 2 * i + h
                rate = rate_ref[s, t]
                tail = jnp.where(row4 == 1, rate, jnp.where(row4 < 3, 1.0, 0.0)).astype(F32)
                parts += [shock_ref[s, t], tail]
            x = jnp.concatenate(parts, axis=0).T
            high = x.astype(BF16)
            low = (x - high.astype(F32)).astype(BF16)
            both = jnp.concatenate([high, low], axis=1)
            e = jnp.dot(both, weight_ref[0], preferred_element_type=F32)
            e = e + jnp.dot(both, weight_ref[1], preferred_element_type=F32)
            d = jnp.exp(e)
            dh = d.astype(BF16)
            dl = (d - dh.astype(F32)).astype(BF16)
            for h in range(2):
                rows = pl.ds(pl.multiple_of((2 * i + h) * paths, paths), paths)
                lhs[t, rows, 0 : 2 * pad] = dh[:, 2 * pad * h : 2 * pad * (h + 1)]
                lhs[t, rows, 2 * pad : 4 * pad] = dl[:, 2 * pad * h : 2 * pad * (h + 1)]
            return carry

        lax.fori_loop(0, scen // 2, body, 0)

    def coefficients(t):
        def body(m, carry):
            coef[m] = jnp.dot(lhs[t], gmat[m], preferred_element_type=F32)
            return carry

        lax.fori_loop(0, terms, body, 0)

        def body2(s, carry):
            rows = pl.ds(pl.multiple_of(s * paths, paths), paths)
            inverse[rows, :] = 1.0 / coef[0, rows, :]
            return carry

        lax.fori_loop(0, scen, body2, 0)

    def evaluate(t, r):
        for s in range(scen):
            rows = slice(s * paths, (s + 1) * paths)
            rung = rung_ref[s, t].astype(F32)
            top = (0.01 + 0.005 * rung) * (1.0 / TOP_INDEX)
            scale = top * 2.5
            shift = (0.9 + 0.1 * rung) * scale
            for c in range(0, lanes, 128):
                cols = slice(c, c + 128)
                y = (hold[slice(s, s + 1), cols] * scale) * inverse[rows, cols] - shift
                y = jnp.minimum(jnp.maximum(y, 0.0), top)
                v = coef[terms - 1, rows, cols]
                for m in range(terms - 2, -1, -1):
                    v = v * y + coef[m, rows, cols]
                vals[t, rows, cols] = v
                out = jnp.sum(v, axis=0, keepdims=True)
                if c + 128 > cohorts:
                    here = c + lax.broadcasted_iota(jnp.int32, (1, 128), 1) < cohorts
                    out = jnp.where(here, out, jnp.sum(y, axis=0, keepdims=True))
                send[r, slice(s, s + 1), cols] = out

    def shortfalls(t, r, mean_scr):
        for s in range(scen):
            rows = slice(s * paths, (s + 1) * paths)
            for c in range(0, lanes, 128):
                cols = slice(c, c + 128)
                short = jnp.minimum(vals[t, rows, cols] - mean_scr[slice(s, s + 1), cols], 0.0)
                send[r, slice(s, s + 1), cols] = jnp.sum(short * short, axis=0, keepdims=True)

    def mine(full):
        return pltpu.roll(full, lax.rem(lanes - own * me, lanes), 1)[:, :own]

    hold[...] = jnp.zeros_like(hold)
    hold[:, 0:own] = capital_ref[...]
    send[0] = pltpu.roll(hold[...], own * me, 1)

    cash = jnp.concatenate([flow_ref[...], jnp.zeros((pad - years, cohorts), F32)], axis=0)
    p0 = cash.astype(BF16)
    rest = cash - p0.astype(F32)
    p1 = rest.astype(BF16)
    p2 = (rest - p1.astype(F32)).astype(BF16)
    ids = lax.broadcasted_iota(jnp.int32, (cohorts, lanes), 0)
    slot = lax.broadcasted_iota(jnp.int32, (cohorts, lanes), 1)
    owner_row = jnp.concatenate([owner_ref[...], jnp.zeros((1, lanes - cohorts), jnp.int32)], axis=1)
    picker = jnp.where((ids == owner_row) | (slot >= cohorts), 1.0, 0.0).astype(BF16)
    flows = jnp.dot(p0, picker, preferred_element_type=F32)
    flows = flows + jnp.dot(p1, picker, preferred_element_type=F32)
    flows = flows + jnp.dot(p2, picker, preferred_element_type=F32)
    for m in range(terms):
        for c in range(0, lanes, 128):
            g = flows[:, c : c + 128] * growth_ref[m]
            gh = g.astype(BF16)
            gl = (g - gh.astype(F32)).astype(BF16)
            for q in range(2):
                gmat[m, 2 * pad * q : 2 * pad * q + pad, c : c + 128] = gh
                gmat[m, 2 * pad * q + pad : 2 * pad * (q + 1), c : c + 128] = gl

    pl.semaphore_wait(barrier, n_in - 1 + n_out - 1)
    start(0)
    for t in range(dates):
        discounts(t)
    coefficients(0)
    set_hold(finish(0))
    means = []
    funds = []
    for t in range(dates):
        r = 1 + t
        evaluate(t, r)
        start(r)
        if t + 1 < dates:
            coefficients(t + 1)
        if t > 0:
            shortfalls(t - 1, dates + t, hold)
            start(dates + t)
        sums = finish(r)
        mean = jnp.where(is_slot, sums / total, 0.0)
        means.append(mean)
        funds.append((sums[:, cohorts : cohorts + 1] / total) * (100.0 * TOP_INDEX))
        set_hold(mean)
    shortfalls(dates - 1, 2 * dates, hold)
    start(2 * dates)

    for t in range(dates):
        sum_send[t : t + 1, :] = jnp.sum(means[t], axis=0, keepdims=True)

    def outer_copy(o):
        return pltpu.make_async_remote_copy(
            src_ref=sum_send,
            dst_ref=sum_recv.at[me_out],
            send_sem=osend_sem.at[o - 1],
            recv_sem=orecv_sem.at[o - 1],
            device_id={"outer": lax.rem(me_out + o, n_out)},
            device_id_type=MESH,
        )

    for o in range(1, n_out):
        outer_copy(o).start()
    sum_recv[me_out] = sum_send[...]

    for t in range(dates):
        fund_ref[:, t : t + 1] = funds[t]
        part = mine(means[t])
        for s in range(scen):
            value_ref[s, t : t + 1, :] = part[s : s + 1]
    for o in range(1, n_out):
        outer_copy(o).wait_recv()
    summed = sum_recv[0]
    for i in range(1, n_out):
        summed = summed + sum_recv[i]
    summary_ref[...] = mine(summed / (scen * n_out))[0:dates]
    for t in range(dates):
        part = mine(jnp.sqrt(finish(dates + 1 + t) / total + EPSILON))
        for s in range(scen):
            down_ref[s, t : t + 1, :] = part[s : s + 1]
    for r in range(2 * dates + 1):
        for o in range(1, n_in):
            inner_copy(r, o).wait_send()
    for o in range(1, n_out):
        outer_copy(o).wait_send()


def shards(n_in, n_out, shocks, node_rate, ladder_rung, cash_flows, owner_map, capital):
    scen, dates, years, paths = shocks.shape
    cohorts = cash_flows.shape[1]
    own = capital.shape[1]
    pad = 64
    lanes = -(-(cohorts + 1) // 128) * 128
    weight = discount_table(years, pad)
    growth = growth_table(years, pad)
    terms = growth.shape[0]
    vmem = pl.BlockSpec(memory_space=pltpu.VMEM)
    smem = pl.BlockSpec(memory_space=pltpu.SMEM)
    rounds = 2 * dates + 1
    rows = scen * paths
    return pl.pallas_call(
        partial(kernel, n_in, n_out, years, pad, cohorts, lanes, terms),
        out_shape=(
            jax.ShapeDtypeStruct((scen, dates, own), F32),
            jax.ShapeDtypeStruct((scen, dates, own), F32),
            jax.ShapeDtypeStruct((scen, dates), F32),
            jax.ShapeDtypeStruct((dates, own), F32),
        ),
        in_specs=[smem, smem] + [vmem] * 6,
        out_specs=(vmem,) * 4,
        scratch_shapes=[
            pltpu.VMEM((dates, rows, 4 * pad), BF16),
            pltpu.VMEM((terms, 4 * pad, lanes), BF16),
            pltpu.VMEM((terms, rows, lanes), F32),
            pltpu.VMEM((rows, lanes), F32),
            pltpu.VMEM((dates, rows, lanes), F32),
            pltpu.VMEM((scen, lanes), F32),
            pltpu.VMEM((rounds, scen, lanes), F32),
            pltpu.VMEM((rounds, n_in, scen, lanes), F32),
            pltpu.VMEM((8, lanes), F32),
            pltpu.VMEM((n_out, 8, lanes), F32),
            pltpu.SemaphoreType.DMA((rounds, n_in)),
            pltpu.SemaphoreType.DMA((rounds, n_in)),
            pltpu.SemaphoreType.DMA((n_out,)),
            pltpu.SemaphoreType.DMA((n_out,)),
        ],
        compiler_params=pltpu.CompilerParams(
            collective_id=0, has_side_effects=True, vmem_limit_bytes=48 * 1024 * 1024
        ),
    )(node_rate, ladder_rung, shocks, cash_flows, owner_map.reshape(1, cohorts), capital, weight, growth)


def solution(mesh):
    return jax.shard_map(
        partial(shards, mesh.shape["inner"], mesh.shape["outer"]),
        mesh=mesh,
        in_specs=(
            P("outer", None, None, "inner"),
            P("outer", None),
            P("outer", None),
            P(),
            P(),
            P("outer", "inner"),
        ),
        out_specs=(
            P("outer", None, "inner"),
            P("outer", None, "inner"),
            P("outer", None),
            P(None, "inner"),
        ),
        check_vma=False,
    )
```

time: 207 us -> 30.9 us (0.15)
  local copies, waits for them, and re-layouts: 69.4 us -> 4.99 us
  blocking collectives: 64.2 us -> 0 us
  other arithmetic: 39.9 us -> 0 us
  Pallas kernels: 0 us -> 25 us
  waiting for transfers between devices: 20.5 us -> 0 us
  starting transfers between devices: 8.17 us -> 0 us
  matrix products: 3.07 us -> 0 us
    dynamic_update_slice x16 -> x0, local copies, waits for them, and re-layouts: 63.3 us -> none  [shards(): lax.map(partial(scenario_value, slot_flows), (discounts, cohort_index))]
    reduce_sum x25 -> x0, other arithmetic: 37 us -> none  [the longest x16 35.6 us: scenario_value(): jnp.sum(slot_flows[:, :, None] * disc_one[:, None, :] * growth, axis=0)]
    psum x2 -> x0, blocking collectives: 34.4 us -> none  [the longest x1 24.5 us: shards(): fund_terms.append(lax.psum(fund_share, 'inner'))]
    all_gather x2 -> x0, blocking collectives: 29.8 us -> none  [the longest x1 15.8 us: shards(): holdings = lax.all_gather(capital, 'inner', axis=1, tiled=True)]
    pallas_call x0 -> x1, Pallas kernels: none -> 25 us  [shards(): pl.pallas_call(partial(kernel, n_in, n_out, years, pad, cohorts, lanes, t...]
    all_to_all x2 -> x0, waiting for transfers between devices: 20.5 us -> none  [shards(): lax.all_to_all(indexed, 'inner', split_axis=1, concat_axis=2, tiled=True)]
    all_to_all x2 -> x0, starting transfers between devices: 8.17 us -> none  [shards(): lax.all_to_all(indexed, 'inner', split_axis=1, concat_axis=2, tiled=True)]
    dot_general x5 -> x0, matrix products: 3.07 us -> none  [the longest x2 1.95 us: shards(): jnp.einsum('kc,skp->scp', slot_flows, discounts, precision=lax.Precision....]
  transfers between devices with their start and end apart: 2 -> 0, of which waited for: 1 -> 0; matrix products, arithmetic and copies ran while one was open for 1% -> 0% of each run, Pallas kernels for 0% -> 0%
where the time goes in v1:
time: 30.9 us; the launch traced here: 30.7 us
  Pallas kernels  25 us (81%)
  local copies, waits for them, and re-layouts  4.99 us (16%)
  between operations  0.71 us (2%)
    pallas_call x1, Pallas kernels, shards(): pl.pallas_call(partial(kernel, n_in, n_out, years, pad, cohorts, lanes, t...  25 us
    unnamed x20, local copies, waits for them, and re-layouts  4.35 us
    pallas_call x1, local copies, waits for them, and re-layouts, shards(): pl.pallas_call(partial(kernel, n_in, n_out, years, pad, cohorts, lanes, t...  0.64 us

profile of v1, /device:TPU:0, one launch (start us, length us, event | category | flops | bytes accessed | tf_op | source)
XLA Modules:
  0.0 30.7 jit_solution(18101388727336161506)
XLA Ops:
  0.6 0.0 copy-start.5
  0.6 0.7 %copy-done.5 = f32[8,2]{0,1:T(2,128)S(1)} copy-done((f32[8,2]{0,1:T(2,128)S(1)}, f32[8,2]{0,1:T(2,128)}, u32[]{:S(2)}) %copy-start.5) | copy-done | bytes 88
  1.3 0.0 copy-start.6
  1.3 0.1 copy.12.rate_ref
  1.4 0.6 %copy-done.6 = s32[8,2]{0,1:T(2,128)S(1)} copy-done((s32[8,2]{0,1:T(2,128)S(1)}, s32[8,2]{0,1:T(2,128)}, u32[]{:S(2)}) %copy-start.6) | copy-done | bytes 88
  2.0 0.1 copy.13.rung_ref
  2.1 0.0 copy-start
  2.1 0.0 copy-start.1
  2.1 0.0 copy-start.2
  2.1 0.0 copy-start.3
  2.1 0.0 copy-start.4
  2.1 1.1 %copy.14.shock_ref = f32[8,2,60,128]{3,2,1,0:T(8,128)S(1)} copy(f32[8,2,60,128]{3,1,2,0:T(2,128)} %param.8) | data formatting | bytes 983040 | tf_op args[0]
  3.2 0.0 copy-done
  3.3 0.0 copy-done.1
  3.3 0.0 copy-done.2
  3.3 0.0 copy-done.3
  3.3 0.0 copy-done.4
  3.3 25.0 %shard_map.111 = (f32[8,2,24]{2,1,0:T(2,128)S(1)}, f32[8,2,24]{2,1,0:T(2,128)S(1)}, f32[8,2]{1,0:T(8,128)S(1)}, f32[2,24]{1,0:T(2,128)S(1)}) custom-call(f32[8,2]{1,0:T(8,128)S(1)} %copy.12.rate_ref, s32[8,2]{1,0:T(8,128)S(1)} %copy.13.rung_ref, f32[8,2,60,128]{3,2,1,0:T(8,128)S(1)} %copy.14.shock_ref, f32[60,192]{1,0:T(8,128)S(1)} %copy-done.2, ...), custom_call_target="tpu_custom_call" | custom-call | tf_op jit(solution)/shard_map/pallas_call | solution.py:303
  28.3 0.6 %copy.15 = f32[8,2]{0,1:T(2,128)} copy(f32[8,2]{1,0:T(8,128)S(1)} %get-tuple-element.6) | data formatting | bytes 128 | tf_op jit(solution)/shard_map/pallas_call | solution.py:303
  29.0 0.6 %copy.19 = f32[8,2,24]{2,1,0:T(2,128)} copy(f32[8,2,24]{2,1,0:T(2,128)S(1)} %get-tuple-element.12) | data formatting | bytes 3072
  29.6 0.6 %copy.20 = f32[8,2,24]{2,1,0:T(2,128)} copy(f32[8,2,24]{2,1,0:T(2,128)S(1)} %get-tuple-element.13) | data formatting | bytes 3072
  30.2 0.6 %copy.21 = f32[2,24]{1,0:T(2,128)} copy(f32[2,24]{1,0:T(2,128)S(1)} %get-tuple-element.15) | data formatting | bytes 384
Async XLA Ops:
  0.6 0.7 %copy-start.5 = (f32[8,2]{0,1:T(2,128)S(1)}, f32[8,2]{0,1:T(2,128)}, u32[]{:S(2)}) copy-start(f32[8,2]{0,1:T(2,128)} %param.9) | copy-start | bytes 196
  1.3 0.7 %copy-start.6 = (s32[8,2]{0,1:T(2,128)S(1)}, s32[8,2]{0,1:T(2,128)}, u32[]{:S(2)}) copy-start(s32[8,2]{0,1:T(2,128)} %param.10) | copy-start | bytes 196
  2.1 1.2 %copy-start = (f32[8,64,128]{2,1,0:T(8,128)S(1)}, f32[8,64,128]{2,1,0:T(8,128)}, u32[]{:S(2)}) copy-start(f32[8,64,128]{2,1,0:T(8,128)} %constant.5.clone.growth_ref) | copy-start | bytes 786436
  2.1 1.2 %copy-start.1 = (bf16[2,256,256]{2,1,0:T(8,128)(2,1)S(1)}, bf16[2,256,256]{2,1,0:T(8,128)(2,1)}, u32[]{:S(2)}) copy-start(bf16[2,256,256]{2,1,0:T(8,128)(2,1)} %constant.4.clone.weight_ref) | copy-start | bytes 786436
  2.1 1.2 %copy-start.2 = (f32[60,192]{1,0:T(8,128)S(1)}, f32[60,192]{1,0:T(8,128)}, u32[]{:S(2)}) copy-start(f32[60,192]{1,0:T(8,128)} %flow_ref.1) | copy-start | bytes 138244
  2.1 1.2 %copy-start.3 = (f32[8,24]{1,0:T(8,128)S(1)}, f32[8,24]{1,0:T(8,128)}, u32[]{:S(2)}) copy-start(f32[8,24]{1,0:T(8,128)} %capital_ref.1) | copy-start | bytes 2308
  2.1 1.2 %copy-start.4 = (s32[192]{0:T(256)S(1)}, s32[192]{0:T(256)}, u32[]{:S(2)}) copy-start(s32[192]{0:T(256)} %param.12) | copy-start | bytes 2308

commit v2 on v1

--- a/solution.py
+++ b/solution.py
@@ -26,7 +26,7 @@
     return high, low
 
 
-def discount_table(years, pad):
+def discount_table(years, dates, pad):
     decay = 1.0 - REVERT
     year = np.arange(years, dtype=np.float64)
     weights = np.where(
@@ -36,21 +36,19 @@
     )
     count = year + 1.0
     ramp = decay * (1.0 - decay**count) / REVERT
-    one = np.zeros((pad, pad))
-    one[:years, :years] = -VOLATILITY * weights
-    one[years, :years] = -LONG_LEVEL * (count - ramp)
-    one[years + 1, :years] = -ramp
+    used = years * dates
+    one = np.zeros((2 * pad, 2 * pad * dates))
+    for t in range(dates):
+        for copy in (0, pad):
+            cols = slice(2 * pad * t + copy, 2 * pad * t + copy + years)
+            one[t:used:dates, cols] = -VOLATILITY * weights
+            one[used, cols] = -LONG_LEVEL * (count - ramp)
+            one[used + 2 + t, cols] = -ramp
     high, low = split_bf16(one)
     rest = one - high.astype(np.float64) - low.astype(np.float64)
-    one[years + 2] = rest[years]
+    one[used + 1] = rest[used]
     high, low = split_bf16(one)
-    full = np.zeros((2, 4 * pad, 4 * pad), ml_dtypes.bfloat16)
-    for which, part in enumerate((high, low)):
-        for row in (0, 2 * pad):
-            for copy in (0, pad):
-                full[which, row : row + pad, copy : copy + pad] = part
-                full[which, row + pad : row + 2 * pad, 2 * pad + copy : 3 * pad + copy] = part
-    return full
+    return np.stack([high, low])
 
 
 def growth_table(years, pad):
@@ -73,29 +71,41 @@
             found = found * probe[None, :] + table[m][:, None]
         if np.max(np.abs(found / exact - 1.0)) < 2.0**-25:
             break
-    out = np.zeros((degree + 1, pad, 128), np.float32)
-    out[:, :years] = table[:, :, None]
-    return out
+    out = np.zeros((pad, 128), np.float32)
+    out[:years, : degree + 1] = table.T
+    return out, degree + 1
 
 
 def kernel(
     n_in, n_out, years, pad, cohorts, lanes, terms,
+    rate_hbm, rung_hbm, shock_hbm, flow_hbm, owner_hbm, capital_hbm, weight_hbm, growth_hbm,
+    value_ref, down_ref, fund_ref, summary_ref,
     rate_ref, rung_ref, shock_ref, flow_ref, owner_ref, capital_ref, weight_ref, growth_ref,
-    value_ref, down_ref, fund_ref, summary_ref,
-    lhs, gmat, coef, inverse, vals, hold, send, recv, sum_send, sum_recv,
-    send_sem, recv_sem, osend_sem, orecv_sem,
+    lhs, gmat, coef, inverse, vals, hold, send, recv, short, short_send, short_recv, sum_send, sum_recv,
+    load_sem, send_sem, recv_sem, ssend_sem, srecv_sem, osend_sem, orecv_sem,
 ):
-    scen, dates, _, paths = shock_ref.shape
-    own = capital_ref.shape[1]
+    dates, scen = rate_hbm.shape
+    paths = shock_hbm.shape[1]
+    used = dates * years
+    own = capital_hbm.shape[1]
     total = paths * n_in
     me = lax.axis_index("inner")
     me_out = lax.axis_index("outer")
+    loads = [
+        pltpu.make_async_copy(source, target, load_sem.at[i])
+        for i, (source, target) in enumerate((
+            (capital_hbm, capital_ref), (flow_hbm, flow_ref), (owner_hbm, owner_ref), (growth_hbm, growth_ref),
+            (rate_hbm, rate_ref), (weight_hbm, weight_ref), (shock_hbm, shock_ref), (rung_hbm, rung_ref),
+        ))
+    ]
     barrier = pltpu.get_barrier_semaphore()
     for o in range(1, n_in):
         pl.semaphore_signal(barrier, 1, device_id={"inner": lax.rem(me + o, n_in)}, device_id_type=MESH)
     for o in range(1, n_out):
         pl.semaphore_signal(barrier, 1, device_id={"outer": lax.rem(me_out + o, n_out)}, device_id_type=MESH)
 
+    for load in loads:
+        load.start()
     lane = lax.broadcasted_iota(jnp.int32, (scen, lanes), 1)
     is_slot = lane < cohorts
 
@@ -126,50 +136,42 @@
         fund = jnp.sum(jnp.where(is_slot, held, 0.0), axis=1, keepdims=True)
         hold[...] = jnp.where(is_slot, held, fund)
 
-    def discounts(t):
-        def body(i, carry):
-            row4 = lax.broadcasted_iota(jnp.int32, (pad - years, paths), 0)
-            parts = []
-            for h in range(2):
-                s = 2 * i + h
-                rate = rate_ref[s, t]
-                tail = jnp.where(row4 == 1, rate, jnp.where(row4 < 3, 1.0, 0.0)).astype(F32)
-                parts += [shock_ref[s, t], tail]
-            x = jnp.concatenate(parts, axis=0).T
+    def discounts():
+        weights = [jnp.concatenate([weight_ref[i], weight_ref[i]], axis=0) for i in range(2)]
+        row8 = lax.broadcasted_iota(jnp.int32, (2 * pad - used, paths), 0)
+        for s in range(scen):
+            tail = jnp.where(row8 < 2, 1.0, 0.0).astype(F32)
+            for t in range(dates):
+                tail = jnp.where(row8 == 2 + t, rate_ref[t, s], tail)
+            x = jnp.concatenate([shock_ref[s * used : (s + 1) * used, :], tail], axis=0).T
             high = x.astype(BF16)
             low = (x - high.astype(F32)).astype(BF16)
             both = jnp.concatenate([high, low], axis=1)
-            e = jnp.dot(both, weight_ref[0], preferred_element_type=F32)
-            e = e + jnp.dot(both, weight_ref[1], preferred_element_type=F32)
+            e = jnp.dot(both, weights[0], preferred_element_type=F32)
+            e = e + jnp.dot(both, weights[1], preferred_element_type=F32)
             d = jnp.exp(e)
             dh = d.astype(BF16)
             dl = (d - dh.astype(F32)).astype(BF16)
-            for h in range(2):
-                rows = pl.ds(pl.multiple_of((2 * i + h) * paths, paths), paths)
-                lhs[t, rows, 0 : 2 * pad] = dh[:, 2 * pad * h : 2 * pad * (h + 1)]
-                lhs[t, rows, 2 * pad : 4 * pad] = dl[:, 2 * pad * h : 2 * pad * (h + 1)]
-            return carry
-
-        lax.fori_loop(0, scen // 2, body, 0)
+            rows = slice(s * paths, (s + 1) * paths)
+            for t in range(dates):
+                lhs[t, rows, 0 : 2 * pad] = dh[:, 2 * pad * t : 2 * pad * (t + 1)]
+                lhs[t, rows, 2 * pad : 4 * pad] = dl[:, 2 * pad * t : 2 * pad * (t + 1)]
 
     def coefficients(t):
-        def body(m, carry):
+        for m in range(terms):
             coef[m] = jnp.dot(lhs[t], gmat[m], preferred_element_type=F32)
-            return carry
-
-        lax.fori_loop(0, terms, body, 0)
-
-        def body2(s, carry):
-            rows = pl.ds(pl.multiple_of(s * paths, paths), paths)
-            inverse[rows, :] = 1.0 / coef[0, rows, :]
-            return carry
-
-        lax.fori_loop(0, scen, body2, 0)
+            if m == 0:
+                for s in range(scen):
+                    rows = slice(s * paths, (s + 1) * paths)
+                    nominal = coef[0, rows, :]
+                    guess = pl.reciprocal(nominal, approx=True)
+                    guess = guess * (2.0 - nominal * guess)
+                    inverse[rows, :] = guess * (2.0 - nominal * guess)
 
     def evaluate(t, r):
         for s in range(scen):
             rows = slice(s * paths, (s + 1) * paths)
-            rung = rung_ref[s, t].astype(F32)
+            rung = rung_ref[t, s].astype(F32)
             top = (0.01 + 0.005 * rung) * (1.0 / TOP_INDEX)
             scale = top * 2.5
             shift = (0.9 + 0.1 * rung) * scale
@@ -187,17 +189,36 @@
                     out = jnp.where(here, out, jnp.sum(y, axis=0, keepdims=True))
                 send[r, slice(s, s + 1), cols] = out
 
-    def shortfalls(t, r, mean_scr):
+    def short_copy(t, o):
+        return pltpu.make_async_remote_copy(
+            src_ref=short_send.at[t, o - 1],
+            dst_ref=short_recv.at[t, me],
+            send_sem=ssend_sem.at[t, o - 1],
+            recv_sem=srecv_sem.at[t, o - 1],
+            device_id={"inner": lax.rem(me + o, n_in)},
+            device_id_type=MESH,
+        )
+
+    def shortfalls(t):
         for s in range(scen):
             rows = slice(s * paths, (s + 1) * paths)
             for c in range(0, lanes, 128):
                 cols = slice(c, c + 128)
-                short = jnp.minimum(vals[t, rows, cols] - mean_scr[slice(s, s + 1), cols], 0.0)
-                send[r, slice(s, s + 1), cols] = jnp.sum(short * short, axis=0, keepdims=True)
+                below = jnp.minimum(vals[t, rows, cols] - hold[s : s + 1, cols], 0.0)
+                short[s : s + 1, cols] = jnp.sum(below * below, axis=0, keepdims=True)
+        for o in range(1, n_in):
+            short_send[t, o - 1] = of_device(short[...], lax.rem(me + o, n_in))
+            short_copy(t, o).start()
+        short_recv[t, me] = of_device(short[...], me)
+
+    def of_device(full, device):
+        return pltpu.roll(full, lax.rem(lanes - own * device, lanes), 1)[:, :128]
 
     def mine(full):
-        return pltpu.roll(full, lax.rem(lanes - own * me, lanes), 1)[:, :own]
-
+        return of_device(full, me)[:, :own]
+
+    for load in loads[:4]:
+        load.wait()
     hold[...] = jnp.zeros_like(hold)
     hold[:, 0:own] = capital_ref[...]
     send[0] = pltpu.roll(hold[...], own * me, 1)
@@ -216,7 +237,7 @@
     flows = flows + jnp.dot(p2, picker, preferred_element_type=F32)
     for m in range(terms):
         for c in range(0, lanes, 128):
-            g = flows[:, c : c + 128] * growth_ref[m]
+            g = flows[:, c : c + 128] * growth_ref[:, m : m + 1]
             gh = g.astype(BF16)
             gl = (g - gh.astype(F32)).astype(BF16)
             for q in range(2):
@@ -225,8 +246,9 @@
 
     pl.semaphore_wait(barrier, n_in - 1 + n_out - 1)
     start(0)
-    for t in range(dates):
-        discounts(t)
+    for load in loads[4:]:
+        load.wait()
+    discounts()
     coefficients(0)
     set_hold(finish(0))
     means = []
@@ -238,15 +260,13 @@
         if t + 1 < dates:
             coefficients(t + 1)
         if t > 0:
-            shortfalls(t - 1, dates + t, hold)
-            start(dates + t)
+            shortfalls(t - 1)
         sums = finish(r)
         mean = jnp.where(is_slot, sums / total, 0.0)
         means.append(mean)
-        funds.append((sums[:, cohorts : cohorts + 1] / total) * (100.0 * TOP_INDEX))
+        funds.append((sums[:, cohorts : cohorts + 1] / total).T * (100.0 * TOP_INDEX))
         set_hold(mean)
-    shortfalls(dates - 1, 2 * dates, hold)
-    start(2 * dates)
+    shortfalls(dates - 1)
 
     for t in range(dates):
         sum_send[t : t + 1, :] = jnp.sum(means[t], axis=0, keepdims=True)
@@ -266,7 +286,7 @@
     sum_recv[me_out] = sum_send[...]
 
     for t in range(dates):
-        fund_ref[:, t : t + 1] = funds[t]
+        fund_ref[t : t + 1, :] = funds[t]
         part = mine(means[t])
         for s in range(scen):
             value_ref[s, t : t + 1, :] = part[s : s + 1]
@@ -277,12 +297,19 @@
         summed = summed + sum_recv[i]
     summary_ref[...] = mine(summed / (scen * n_out))[0:dates]
     for t in range(dates):
-        part = mine(jnp.sqrt(finish(dates + 1 + t) / total + EPSILON))
+        for o in range(1, n_in):
+            short_copy(t, o).wait_recv()
+        squares = short_recv[t, 0]
+        for i in range(1, n_in):
+            squares = squares + short_recv[t, i]
+        part = jnp.sqrt(squares[:, :own] / total + EPSILON)
         for s in range(scen):
             down_ref[s, t : t + 1, :] = part[s : s + 1]
-    for r in range(2 * dates + 1):
-        for o in range(1, n_in):
+    for o in range(1, n_in):
+        for r in range(dates + 1):
             inner_copy(r, o).wait_send()
+        for t in range(dates):
+            short_copy(t, o).wait_send()
     for o in range(1, n_out):
         outer_copy(o).wait_send()
 
@@ -293,24 +320,32 @@
     own = capital.shape[1]
     pad = 64
     lanes = -(-(cohorts + 1) // 128) * 128
-    weight = discount_table(years, pad)
-    growth = growth_table(years, pad)
-    terms = growth.shape[0]
+    weight = discount_table(years, dates, pad)
+    growth, terms = growth_table(years, pad)
+    by_year = jnp.transpose(shocks, (0, 2, 1, 3)).reshape(scen * years * dates, paths)
     vmem = pl.BlockSpec(memory_space=pltpu.VMEM)
-    smem = pl.BlockSpec(memory_space=pltpu.SMEM)
-    rounds = 2 * dates + 1
+    hbm = pl.BlockSpec(memory_space=pltpu.HBM)
+    rounds = dates + 1
     rows = scen * paths
-    return pl.pallas_call(
+    results = pl.pallas_call(
         partial(kernel, n_in, n_out, years, pad, cohorts, lanes, terms),
         out_shape=(
             jax.ShapeDtypeStruct((scen, dates, own), F32),
             jax.ShapeDtypeStruct((scen, dates, own), F32),
-            jax.ShapeDtypeStruct((scen, dates), F32),
+            jax.ShapeDtypeStruct((dates, scen), F32),
             jax.ShapeDtypeStruct((dates, own), F32),
         ),
-        in_specs=[smem, smem] + [vmem] * 6,
+        in_specs=[hbm] * 8,
         out_specs=(vmem,) * 4,
         scratch_shapes=[
+            pltpu.SMEM((dates, scen), F32),
+            pltpu.SMEM((dates, scen), jnp.int32),
+            pltpu.VMEM(by_year.shape, F32),
+            pltpu.VMEM((years, cohorts), F32),
+            pltpu.VMEM((1, cohorts), jnp.int32),
+            pltpu.VMEM((scen, own), F32),
+            pltpu.VMEM(weight.shape, BF16),
+            pltpu.VMEM(growth.shape, F32),
             pltpu.VMEM((dates, rows, 4 * pad), BF16),
             pltpu.VMEM((terms, 4 * pad, lanes), BF16),
             pltpu.VMEM((terms, rows, lanes), F32),
@@ -319,17 +354,41 @@
             pltpu.VMEM((scen, lanes), F32),
             pltpu.VMEM((rounds, scen, lanes), F32),
             pltpu.VMEM((rounds, n_in, scen, lanes), F32),
+            pltpu.VMEM((scen, lanes), F32),
+            pltpu.VMEM((dates, n_in, scen, 128), F32),
+            pltpu.VMEM((dates, n_in, scen, 128), F32),
             pltpu.VMEM((8, lanes), F32),
             pltpu.VMEM((n_out, 8, lanes), F32),
+            pltpu.SemaphoreType.DMA((8,)),
             pltpu.SemaphoreType.DMA((rounds, n_in)),
             pltpu.SemaphoreType.DMA((rounds, n_in)),
+            pltpu.SemaphoreType.DMA((dates, n_in)),
+            pltpu.SemaphoreType.DMA((dates, n_in)),
             pltpu.SemaphoreType.DMA((n_out,)),
             pltpu.SemaphoreType.DMA((n_out,)),
         ],
         compiler_params=pltpu.CompilerParams(
-            collective_id=0, has_side_effects=True, vmem_limit_bytes=48 * 1024 * 1024
+            collective_id=0, has_side_effects=True, vmem_limit_bytes=55168 * 1024
         ),
-    )(node_rate, ladder_rung, shocks, cash_flows, owner_map.reshape(1, cohorts), capital, weight, growth)
+    )(node_rate.T, ladder_rung.T, by_year, cash_flows, owner_map.reshape(1, cohorts), capital, weight, growth)
+    value, down, fund, summary = pl.pallas_call(
+        deliver,
+        out_shape=tuple(jax.ShapeDtypeStruct(x.shape, x.dtype) for x in results),
+        in_specs=[pl.BlockSpec(memory_space=pl.ANY)] * 4,
+        out_specs=(pl.BlockSpec(memory_space=pl.ANY),) * 4,
+        scratch_shapes=[pltpu.SemaphoreType.DMA((4,))],
+        compiler_params=pltpu.CompilerParams(vmem_limit_bytes=1024 * 1024),
+    )(*results)
+    return value, down, fund.T, summary
+
+
+def deliver(*refs):
+    count = (len(refs) - 1) // 2
+    copies = [pltpu.make_async_copy(refs[i], refs[count + i], refs[-1].at[i]) for i in range(count)]
+    for copy in copies:
+        copy.start()
+    for copy in copies:
+        copy.wait()
 
 
 def solution(mesh):

time: 30.9 us -> 25.2 us (0.82)
  local copies, waits for them, and re-layouts: 4.99 us -> 0.69 us
  Pallas kernels: 25 us -> 23.7 us
    unnamed x20 -> x8, local copies, waits for them, and re-layouts: 4.35 us -> 0.69 us
    pallas_call x1, Pallas kernels: 25 us -> 23 us  [shards(): pl.pallas_call(partial(kernel, n_in, n_out, years, pad, cohorts, lanes, t...]
    pallas_call x0 -> x1, Pallas kernels: none -> 0.64 us  [shards(): pl.pallas_call(deliver, out_shape=tuple((jax.ShapeDtypeStruct(x.shape, x....]
    pallas_call x1 -> x0, local copies, waits for them, and re-layouts: 0.64 us -> none  [shards(): pl.pallas_call(partial(kernel, n_in, n_out, years, pad, cohorts, lanes, t...]
where the time goes in v2:
time: 25.2 us; the launch traced here: 25 us
  Pallas kernels  23.7 us (94%)
  local copies, waits for them, and re-layouts  0.69 us (3%)
  between operations  0.67 us (3%)
    pallas_call x1, Pallas kernels, shards(): pl.pallas_call(partial(kernel, n_in, n_out, years, pad, cohorts, lanes, t...  23 us
    unnamed x8, local copies, waits for them, and re-layouts  0.69 us
    pallas_call x1, Pallas kernels, shards(): pl.pallas_call(deliver, out_shape=tuple((jax.ShapeDtypeStruct(x.shape, x....  0.64 us

profile of v2, /device:TPU:0, one launch (start us, length us, event | category | flops | bytes accessed | tf_op | source)
XLA Modules:
  0.0 25.0 jit_solution(12797305028902238105)
XLA Ops:
  0.6 0.0 copy-start
  0.6 0.0 copy-start.2
  0.7 0.0 copy-start.3
  0.7 0.0 copy-start.1
  0.7 0.6 %copy-done = f32[8,24]{1,0:T(8,128)S(1)} copy-done((f32[8,24]{1,0:T(8,128)S(1)}, f32[8,24]{1,0:T(8,128)}, u32[]{:S(2)}) %copy-start) | copy-done | bytes 792
  1.3 0.0 copy-done.2
  1.3 0.0 copy-done.3
  1.3 0.0 copy-done.1
  1.4 23.0 %shard_map.111 = (f32[8,2,24]{2,1,0:T(2,128)S(1)}, f32[8,2,24]{2,1,0:T(2,128)S(1)}, f32[2,8]{1,0:T(2,128)S(1)}, f32[2,24]{1,0:T(2,128)S(1)}) custom-call(f32[2,8]{1,0:T(2,128)S(1)} %bitcast.7, s32[2,8]{1,0:T(2,128)S(1)} %bitcast.8, f32[960,128]{1,0:T(8,128)} %bitcast.10, f32[60,192]{1,0:T(8,128)} %flow_hbm.1, s32[1,192]{1,0:T(1,128)S(1)} %bitcast.9, ...), custom_call_target="tpu_custom_call" | custom-call | tf_op jit(solution)/shard_map/pallas_call | solution.py:330
  24.4 0.6 %shard_map.112 = (f32[8,2,24]{2,1,0:T(2,128)}, f32[8,2,24]{2,1,0:T(2,128)}, f32[2,8]{1,0:T(2,128)}, f32[2,24]{1,0:T(2,128)}) custom-call(f32[8,2,24]{2,1,0:T(2,128)S(1)} %get-tuple-element.12.refs_0_, f32[8,2,24]{2,1,0:T(2,128)S(1)} %get-tuple-element.13.refs_1_, f32[2,8]{1,0:T(2,128)S(1)} %get-tuple-element.14.refs_2_, f32[2,24]{1,0:T(2,128)S(1)} %get-tuple-element.15.refs_3_), custom_call_target="tpu_custom_call" | custom-call | tf_op jit(solution)/shard_map/pallas_call | solution.py:374
Async XLA Ops:
  0.6 0.7 %copy-start = (f32[8,24]{1,0:T(8,128)S(1)}, f32[8,24]{1,0:T(8,128)}, u32[]{:S(2)}) copy-start(f32[8,24]{1,0:T(8,128)} %capital_hbm.1) | copy-start | bytes 2308
  0.6 0.7 %copy-start.2 = (s32[8,2]{0,1:T(2,128)S(1)}, s32[8,2]{0,1:T(2,128)}, u32[]{:S(2)}) copy-start(s32[8,2]{0,1:T(2,128)} %param.10) | copy-start | bytes 196
  0.7 0.7 %copy-start.3 = (s32[192]{0:T(256)S(1)}, s32[192]{0:T(256)}, u32[]{:S(2)}) copy-start(s32[192]{0:T(256)} %param.12) | copy-start | bytes 2308
  0.7 0.7 %copy-start.1 = (f32[8,2]{0,1:T(2,128)S(1)}, f32[8,2]{0,1:T(2,128)}, u32[]{:S(2)}) copy-start(f32[8,2]{0,1:T(2,128)} %param.9) | copy-start | bytes 196

commit v3 on v2

--- a/solution.py
+++ b/solution.py
@@ -98,13 +98,14 @@
             (rate_hbm, rate_ref), (weight_hbm, weight_ref), (shock_hbm, shock_ref), (rung_hbm, rung_ref),
         ))
     ]
+    loads[0].start()
     barrier = pltpu.get_barrier_semaphore()
     for o in range(1, n_in):
         pl.semaphore_signal(barrier, 1, device_id={"inner": lax.rem(me + o, n_in)}, device_id_type=MESH)
     for o in range(1, n_out):
         pl.semaphore_signal(barrier, 1, device_id={"outer": lax.rem(me_out + o, n_out)}, device_id_type=MESH)
 
-    for load in loads:
+    for load in loads[1:]:
         load.start()
     lane = lax.broadcasted_iota(jnp.int32, (scen, lanes), 1)
     is_slot = lane < cohorts
@@ -217,12 +218,16 @@
     def mine(full):
         return of_device(full, me)[:, :own]
 
-    for load in loads[:4]:
-        load.wait()
+    loads[0].wait()
     hold[...] = jnp.zeros_like(hold)
     hold[:, 0:own] = capital_ref[...]
     send[0] = pltpu.roll(hold[...], own * me, 1)
 
+    pl.semaphore_wait(barrier, n_in - 1 + n_out - 1)
+    start(0)
+
+    for load in loads[1:4]:
+        load.wait()
     cash = jnp.concatenate([flow_ref[...], jnp.zeros((pad - years, cohorts), F32)], axis=0)
     p0 = cash.astype(BF16)
     rest = cash - p0.astype(F32)
@@ -244,8 +249,6 @@
                 gmat[m, 2 * pad * q : 2 * pad * q + pad, c : c + 128] = gh
                 gmat[m, 2 * pad * q + pad : 2 * pad * (q + 1), c : c + 128] = gl
 
-    pl.semaphore_wait(barrier, n_in - 1 + n_out - 1)
-    start(0)
     for load in loads[4:]:
         load.wait()
     discounts()

time: 25.2 us -> 25.2 us (level)
  no operation moved by 1% of the time
where the time goes in v3:
time: 25.2 us; the launch traced here: 25 us
  Pallas kernels  23.7 us (94%)
  local copies, waits for them, and re-layouts  0.69 us (3%)
  between operations  0.67 us (3%)
    pallas_call x1, Pallas kernels, shards(): pl.pallas_call(partial(kernel, n_in, n_out, years, pad, cohorts, lanes, t...  23 us
    unnamed x8, local copies, waits for them, and re-layouts  0.69 us
    pallas_call x1, Pallas kernels, shards(): pl.pallas_call(deliver, out_shape=tuple((jax.ShapeDtypeStruct(x.shape, x....  0.64 us

profile of v3, /device:TPU:0, one launch (start us, length us, event | category | flops | bytes accessed | tf_op | source)
XLA Modules:
  0.0 25.0 jit_solution(316639839577569393)
XLA Ops:
  0.6 0.0 copy-start
  0.6 0.0 copy-start.2
  0.7 0.0 copy-start.3
  0.7 0.0 copy-start.1
  0.7 0.6 %copy-done = f32[8,24]{1,0:T(8,128)S(1)} copy-done((f32[8,24]{1,0:T(8,128)S(1)}, f32[8,24]{1,0:T(8,128)}, u32[]{:S(2)}) %copy-start) | copy-done | bytes 792
  1.3 0.0 copy-done.2
  1.3 0.0 copy-done.3
  1.3 0.0 copy-done.1
  1.4 23.0 %shard_map.111 = (f32[8,2,24]{2,1,0:T(2,128)S(1)}, f32[8,2,24]{2,1,0:T(2,128)S(1)}, f32[2,8]{1,0:T(2,128)S(1)}, f32[2,24]{1,0:T(2,128)S(1)}) custom-call(f32[2,8]{1,0:T(2,128)S(1)} %bitcast.7, s32[2,8]{1,0:T(2,128)S(1)} %bitcast.8, f32[960,128]{1,0:T(8,128)} %bitcast.10, f32[60,192]{1,0:T(8,128)} %flow_hbm.1, s32[1,192]{1,0:T(1,128)S(1)} %bitcast.9, ...), custom_call_target="tpu_custom_call" | custom-call | tf_op jit(solution)/shard_map/pallas_call | solution.py:333
  24.4 0.6 %shard_map.112 = (f32[8,2,24]{2,1,0:T(2,128)}, f32[8,2,24]{2,1,0:T(2,128)}, f32[2,8]{1,0:T(2,128)}, f32[2,24]{1,0:T(2,128)}) custom-call(f32[8,2,24]{2,1,0:T(2,128)S(1)} %get-tuple-element.12.refs_0_, f32[8,2,24]{2,1,0:T(2,128)S(1)} %get-tuple-element.13.refs_1_, f32[2,8]{1,0:T(2,128)S(1)} %get-tuple-element.14.refs_2_, f32[2,24]{1,0:T(2,128)S(1)} %get-tuple-element.15.refs_3_), custom_call_target="tpu_custom_call" | custom-call | tf_op jit(solution)/shard_map/pallas_call | solution.py:377
Async XLA Ops:
  0.6 0.7 %copy-start = (f32[8,24]{1,0:T(8,128)S(1)}, f32[8,24]{1,0:T(8,128)}, u32[]{:S(2)}) copy-start(f32[8,24]{1,0:T(8,128)} %capital_hbm.1) | copy-start | bytes 2308
  0.6 0.7 %copy-start.2 = (s32[8,2]{0,1:T(2,128)S(1)}, s32[8,2]{0,1:T(2,128)}, u32[]{:S(2)}) copy-start(s32[8,2]{0,1:T(2,128)} %param.10) | copy-start | bytes 196
  0.7 0.7 %copy-start.3 = (s32[192]{0:T(256)S(1)}, s32[192]{0:T(256)}, u32[]{:S(2)}) copy-start(s32[192]{0:T(256)} %param.12) | copy-start | bytes 2308
  0.7 0.7 %copy-start.1 = (f32[8,2]{0,1:T(2,128)S(1)}, f32[8,2]{0,1:T(2,128)}, u32[]{:S(2)}) copy-start(f32[8,2]{0,1:T(2,128)} %param.9) | copy-start | bytes 196
